TPU v7x, 128 devices: a whole 4x4x4 slice. The times are simulated.
128 devices in a mesh: seq: 16 (over z, y), expert: 8 (over x, core).
Axes of the slice: x: 4, y: 4, z: 4, core: 2. Of those that a mesh axis runs over, the one named last changes fastest.
Arguments:
- tokens: bfloat16 [2048, 4096], P(('seq', 'expert')), may hold values from -6 to 6
- gain_mamba: float32 [4096], replicated, may hold values from 0.1 to 1.9
- in_weight: bfloat16 [2, 4096, 8192], P(None, 'seq', 'expert'), may hold values from -0.09375 to 0.09375
- conv_weight: float32 [4, 8192], P(None, 'expert'), may hold values from -3 to 3
- conv_bias: float32 [8192], P('expert'), may hold values from -3 to 3
- xproj_weight: bfloat16 [8192, 288], P('expert'), may hold values from -0.0625 to 0.0625
- dt_weight: bfloat16 [256, 8192], P(None, 'expert'), may hold values from -0.375 to 0.375
- dt_bias: float32 [8192], P('expert'), may hold values from -7 to -2
- a_rate: float32 [16, 8192], P(None, 'expert'), may hold values from 0.01 to 8
- skip_d: float32 [8192], P('expert'), may hold values from 0.5 to 1.5
- out_weight: bfloat16 [8192, 4096], P('expert', 'seq'), may hold values from -0.0625 to 0.0625
- gain_moe: float32 [4096], replicated, may hold values from 0.1 to 1.9
- expert_ids: int32 [2048, 2], P(('seq', 'expert')), may hold values from 0 to 15, all different within a row; in each aligned block of 16 rows (0 to 15, 16 to 31, ...) at most 4 rows name the same one
- gate_weights: float32 [2048, 2], P(('seq', 'expert')), may hold values from 0.2 to 1
- w_gate: bfloat16 [16, 4096, 7168], P('seq', None, 'expert'), may hold values from -0.09375 to 0.09375
- w_up: bfloat16 [16, 4096, 7168], P('seq', None, 'expert'), may hold values from -0.09375 to 0.09375
- w_down: bfloat16 [16, 7168, 4096], P('seq', 'expert'), may hold values from -0.0625 to 0.0625
Outputs:
- mixed: bfloat16 [2048, 4096], P(('seq', 'expert'))
Inputs may be any that keep to these rules, and one draw needn't show every extreme that they name: `expert_ids`: each row names 2 different experts. In each aligned block of 16 rows (the rows of one device) no expert is named by more than 4 rows, a bound that some block reaches.
All inputs are finite; a program needn't handle non-finite values.
Results may differ from a plain program's by a relative error of at most 0.03.
Values may be sent and summed in bfloat16 or wider, within the bound.
A program may use at most 192 MiB of HBM per device.

v0:
```python
import jax
import jax.numpy as jnp
from jax import lax
from jax.sharding import PartitionSpec as P

STATE = 16
CONV = 4
RANK = 256
TOP = 2


def from_behind(block, axis, distance):
    devices = range(lax.axis_size(axis))
    route = [(i - distance, i) for i in devices if i - distance in devices]
    return lax.ppermute(block, axis, route)


def rms_norm(values, gain):
    wide = values.astype(jnp.float32)
    return wide * lax.rsqrt(jnp.mean(wide * wide, axis=-1, keepdims=True) + 1e-05) * gain


def combine_states(earlier, later):
    return (earlier[0] * later[0], later[0] * earlier[1] + later[1])


def per_device(
    tokens,
    gain_mamba,
    in_weight,
    conv_weight,
    conv_bias,
    xproj_weight,
    dt_weight,
    dt_bias,
    a_rate,
    skip_d,
    out_weight,
    gain_moe,
    expert_ids,
    gate_weights,
    w_gate,
    w_up,
    w_down,
):
    rows, dim = tokens.shape
    n_seq = lax.axis_size("seq")
    n_exp = lax.axis_size("expert")
    group = lax.all_gather(tokens, "expert", axis=0, tiled=True)
    local_tok = group.shape[0]
    normed = rms_norm(group, gain_mamba).astype(jnp.bfloat16)
    both = jnp.einsum(
        "td,kdc->tkc",
        normed,
        lax.all_gather(in_weight, "seq", axis=1, tiled=True),
        preferred_element_type=jnp.float32,
    )
    xpart = both[:, 0]
    zpart = both[:, 1]
    edge = from_behind(xpart[local_tok - (CONV - 1) :], "seq", 1)
    padded = jnp.concatenate([edge, xpart], axis=0)
    conv = conv_bias
    for tap in range(CONV):
        conv = conv + conv_weight[tap] * padded[tap : tap + local_tok]
    inner = jax.nn.silu(conv).astype(jnp.bfloat16)
    partial_value = jnp.dot(inner, xproj_weight, preferred_element_type=jnp.float32)
    low_part, edge_part = (
        lax.psum(partial_value[:, :RANK].astype(jnp.bfloat16), "expert").astype(jnp.float32),
        lax.psum(partial_value[:, RANK:].astype(jnp.bfloat16), "expert").astype(jnp.float32),
    )
    dt_low = low_part.astype(jnp.bfloat16)
    bmat = edge_part[:, :STATE]
    cmat = edge_part[:, STATE:]
    step = jax.nn.softplus(jnp.dot(dt_low, dt_weight, preferred_element_type=jnp.float32) + dt_bias)
    inner_f = inner.astype(jnp.float32)
    decay = jnp.exp(-step[:, None, :] * a_rate[None, :, :])
    source = bmat[:, :, None] * (step * inner_f)[:, None, :]
    cumulative, states = lax.associative_scan(combine_states, (decay, source), axis=0)
    total = cumulative[-1]
    final = states[-1]

    def relay(turn, incoming):
        return from_behind((total * incoming + final).astype(jnp.bfloat16), "seq", 1).astype(
            jnp.float32
        )

    arriving = lax.fori_loop(0, n_seq - 1, relay, jnp.zeros_like(final))
    states = states + cumulative * arriving[None, :, :]
    readout = jnp.sum(cmat[:, :, None] * states, axis=1)
    gated = ((readout + skip_d * inner_f) * jax.nn.silu(zpart)).astype(jnp.bfloat16)
    terms = jnp.dot(
        gated,
        lax.all_gather(out_weight, "seq", axis=1, tiled=True),
        preferred_element_type=jnp.float32,
    )
    mixer = lax.psum_scatter(
        terms.astype(jnp.bfloat16), "expert", scatter_dimension=0, tiled=True
    ).astype(jnp.float32)
    resid = (tokens.astype(jnp.float32) + mixer).astype(jnp.bfloat16)
    normed2 = rms_norm(resid, gain_moe).astype(jnp.bfloat16)
    capacity = max(2, 4 * rows // n_seq)
    slots_all = n_seq * capacity
    flat_ids = expert_ids.reshape(-1)
    onehot = (flat_ids[:, None] == jnp.arange(n_seq, dtype=jnp.int32)[None, :]).astype(jnp.int32)
    before = jnp.cumsum(onehot, axis=0) - onehot
    slot = jnp.sum(before * onehot, axis=1)
    target = flat_ids * capacity + slot
    places = target[:, None] == jnp.arange(slots_all, dtype=jnp.int32)[None, :]
    dispatch_mat = jnp.any(places.reshape(rows, TOP, slots_all), axis=1).astype(jnp.bfloat16)
    send = jnp.einsum(
        "rp,rd->pd", dispatch_mat, normed2, preferred_element_type=jnp.float32
    ).astype(jnp.bfloat16)
    received = lax.all_to_all(
        send.reshape(n_seq, capacity, dim), "seq", split_axis=0, concat_axis=0, tiled=True
    )
    pooled = lax.all_gather(
        received.reshape(1, slots_all, dim), "expert", axis=0, tiled=True
    ).reshape(n_exp * slots_all, dim)
    gate = jnp.dot(pooled, w_gate[0], preferred_element_type=jnp.float32)
    upper = jnp.dot(pooled, w_up[0], preferred_element_type=jnp.float32)
    act = (jax.nn.silu(gate) * upper).astype(jnp.bfloat16)
    outputs = lax.psum_scatter(
        jnp.dot(act, w_down[0], preferred_element_type=jnp.float32).astype(jnp.bfloat16),
        "expert",
        scatter_dimension=0,
        tiled=True,
    )
    returned = lax.all_to_all(
        outputs.reshape(n_seq, capacity, dim), "seq", split_axis=0, concat_axis=0, tiled=True
    ).reshape(slots_all, dim)
    weighting = jnp.where(places, gate_weights.reshape(-1)[:, None], 0.0)
    weighting = jnp.sum(weighting.reshape(rows, TOP, slots_all), axis=1)
    moe = jnp.dot(weighting, returned.astype(jnp.float32), precision=lax.Precision.HIGHEST)
    return (resid.astype(jnp.float32) + moe).astype(jnp.bfloat16)


def solution(mesh):
    placed = (
        P(("seq", "expert"), None),
        P(),
        P(None, "seq", "expert"),
        P(None, "expert"),
        P("expert"),
        P("expert", None),
        P(None, "expert"),
        P("expert"),
        P(None, "expert"),
        P("expert"),
        P("expert", "seq"),
        P(),
        P(("seq", "expert"), None),
        P(("seq", "expert"), None),
        P("seq", None, "expert"),
        P("seq", None, "expert"),
        P("seq", "expert", None),
    )
    return jax.shard_map(
        per_device,
        mesh=mesh,
        in_specs=placed,
        out_specs=P(("seq", "expert"), None),
        check_vma=False,
    )
```

profile of v0, /device:TPU:0, one launch (start us, length us, event | category | flops | bytes accessed | tf_op | source)
XLA Modules:
  0.0 908.5 jit_solution(7577490913799089768)
XLA Ops:
  8.9 26.0 %all-gather.5.cloned.1.call-done = bf16[128,4096]{1,0:T(8,128)(2,1)} async-done(((bf16[16,4096]{1,0:T(8,128)(2,1)}), bf16[128,4096]{1,0:T(8,128)(2,1)}) %all-gather.5.cloned.1.call-update) | async-done | bytes 1048592 | tf_op jit(solution)/shard_map/all_gather | solution.py:49
  36.5 111.9 %all-gather.7.cloned.1.call-done = bf16[2,4096,1024]{2,1,0:T(8,128)(2,1)} async-done(((bf16[2,256,1024]{2,1,0:T(8,128)(2,1)}), bf16[2,4096,1024]{2,1,0:T(8,128)(2,1)}) %all-gather.7.cloned.1.call-update) | async-done | bytes 16777232 | tf_op jit(solution)/shard_map/all_gather | solution.py:55
  148.4 8.5 fusion.20
  163.9 14.0 %psum.14 = bf16[128,32]{0,1:T(8,128)(2,1)S(1)} all-reduce(bf16[128,32]{0,1:T(8,128)(2,1)S(1)} %slice.341), channel_id=1, replica_groups=mesh['seq'=16,'expert'=8] {'expert'}, use_global_device_ids=true, to_apply=%region_1.2 | all-reduce | flops 4096 | bytes 16384 | tf_op jit(solution)/shard_map/psum | solution.py:69
  178.7 44.8 %all-reduce.30.cloned.1.call-done = bf16[128,256]{0,1:T(8,128)(2,1)} async-done(((bf16[128,256]{0,1:T(8,128)(2,1)}), bf16[128,256]{0,1:T(8,128)(2,1)}) %all-reduce.30.cloned.1.call-update) | async-done | bytes 65552 | tf_op jit(solution)/shard_map/psum | solution.py:68
  233.5 10.9 %slice_add_fusion = (f32[64,16,1024]{2,1,0:T(8,128)S(1)}, f32[64,16,1024]{2,1,0:T(8,128)}) fusion(f32[128,16,1024]{2,1,0:T(8,128)} %copy-done.3, f32[128,16,1024]{2,1,0:T(8,128)} %copy-done.2), kind=kLoop, calls=%fused_computation.19 | loop fusion | flops 3145728 | bytes 25165824 | tf_op jit(solution)/shard_map/add | solution.py:24
  308.4 7.0 pad.108
  315.3 10.2 %pad.109 = f32[32,16,1024]{2,1,0:T(8,128)} pad(f32[16,16,1024]{2,1,0:T(8,128)} %add.263, f32[]{:T(128)} %constant.13.clone.1), padding=1_0_1x0_0_0x0_0_0 | pad | bytes 3145732 | tf_op jit(solution)/shard_map/pad | solution.py:78
  325.5 10.1 %pad.95 = f32[32,16,1024]{2,1,0:T(8,128)} pad(f32[16,16,1024]{2,1,0:T(8,128)} %add.253, f32[]{:T(128)} %constant.13.clone.1), padding=1_0_1x0_0_0x0_0_0 | pad | bytes 3145732 | tf_op jit(solution)/shard_map/pad | solution.py:78
  337.9 10.2 %pad.94 = f32[32,16,1024]{2,1,0:T(8,128)} pad(f32[16,16,1024]{2,1,0:T(8,128)} %pad_maximum_fusion.4, f32[]{:T(128)} %constant.13.clone.1), padding=0_1_1x0_0_0x0_0_0 | pad | bytes 3145732 | tf_op jit(solution)/shard_map/pad | solution.py:78
  362.0 18.6 %pad.96 = f32[64,16,1024]{2,1,0:T(8,128)} pad(f32[32,16,1024]{2,1,0:T(8,128)} %pad_maximum_fusion.2, f32[]{:T(128)} %constant.13.clone.1), padding=0_1_1x0_0_0x0_0_0 | pad | bytes 6291460 | tf_op jit(solution)/shard_map/pad | solution.py:78
  380.6 12.0 %pad.97 = f32[64,16,1024]{2,1,0:T(8,128)} pad(f32[32,16,1024]{2,1,0:T(8,128)S(1)} %copy-done.16, f32[]{:T(128)} %constant.13.clone.1), padding=1_0_1x0_0_0x0_0_0 | pad | bytes 6291460 | tf_op jit(solution)/shard_map/pad | solution.py:78
  392.5 6.8 add.257
  399.4 35.6 %pad.99 = f32[128,16,1024]{2,1,0:T(8,128)} pad(f32[64,16,1024]{2,1,0:T(8,128)} %add.257, f32[]{:T(128)} %constant.13.clone.1), padding=1_0_1x0_0_0x0_0_0 | pad | bytes 12582916 | tf_op jit(solution)/shard_map/pad | solution.py:78
  436.5 18.6 %pad.110 = f32[64,16,1024]{2,1,0:T(8,128)} pad(f32[32,16,1024]{2,1,0:T(8,128)} %pad_maximum_fusion.3, f32[]{:T(128)} %constant.13.clone.1), padding=0_1_1x0_0_0x0_0_0 | pad | bytes 6291460 | tf_op jit(solution)/shard_map/pad | solution.py:78
  455.1 11.9 %pad.111 = f32[64,16,1024]{2,1,0:T(8,128)} pad(f32[32,16,1024]{2,1,0:T(8,128)S(1)} %copy-done.15, f32[]{:T(128)} %constant.13.clone.1), padding=1_0_1x0_0_0x0_0_0 | pad | bytes 6291460 | tf_op jit(solution)/shard_map/pad | solution.py:78
  467.0 7.1 add.265
  475.6 7.6 fusion.12
  485.7 35.5 %pad.98 = f32[128,16,1024]{2,1,0:T(8,128)} pad(f32[64,16,1024]{2,1,0:T(8,128)} %pad_maximum_fusion, f32[]{:T(128)} %constant.13.clone.1), padding=0_1_1x0_0_0x0_0_0 | pad | bytes 12582916 | tf_op jit(solution)/shard_map/pad | solution.py:78
  521.2 35.5 %pad.113 = f32[128,16,1024]{2,1,0:T(8,128)} pad(f32[64,16,1024]{2,1,0:T(8,128)} %add.265, f32[]{:T(128)} %constant.13.clone.1), padding=1_0_1x0_0_0x0_0_0 | pad | bytes 12582916 | tf_op jit(solution)/shard_map/pad | solution.py:78
  561.5 35.5 %pad.112 = f32[128,16,1024]{2,1,0:T(8,128)} pad(f32[64,16,1024]{2,1,0:T(8,128)} %pad_maximum_fusion.1, f32[]{:T(128)} %constant.13.clone.1), padding=0_1_1x0_0_0x0_0_0 | pad | bytes 12582916 | tf_op jit(solution)/shard_map/pad | solution.py:78
  598.8 107.7 %while.11 = (s32[]{:T(128)}, f32[16,1024]{1,0:T(8,128)S(1)}, f32[16,1024]{1,0:T(8,128)S(1)}, f32[16,1024]{1,0:T(8,128)S(1)}, s32[]{:T(128)}, /*index=5*/s32[]{:T(128)}) while((s32[]{:T(128)}, f32[16,1024]{1,0:T(8,128)S(1)}, f32[16,1024]{1,0:T(8,128)S(1)}, f32[16,1024]{1,0:T(8,128)S(1)}, s32[]{:T(128)}, /*index=5*/s32[]{:T(128)}) %tuple.47), condition=%wide.region_4.5_spmd.clone, body=%wide.region_3.4_spmd.clone.sunk | while | flops 81923 | bytes 458871 | solution.py:87
  642.6 6.5 collective-permute-start
  706.5 14.0 %multiply_reduce_fusion = f32[128,1024]{1,0:T(8,128)S(1)} fusion(f32[128,16,1024]{2,1,0:T(8,128)} %pad.112, f32[128,16,1024]{2,1,0:T(8,128)} %pad.113, f32[128,16,1024]{2,1,0:T(8,128)} %pad.98, f32[128,16,1024]{2,1,0:T(8,128)} %pad.99, f32[16,1024]{1,0:T(8,128)S(1)} %get-tuple-element.27, f32[128,16]{1,0:T(8,128)S(1)} %copy-done.28), kind=kLoop, calls=%fused_computation.3 | loop fusion | flops 12451840 | bytes 34152448 | tf_op jit(solution)/shard_map/reduce_sum | solution.py:89
  727.1 39.7 %reduce-scatter.3.cloned.1.call-done = bf16[16,4096]{1,0:T(8,128)(2,1)} async-done(((bf16[128,4096]{1,0:T(8,128)(2,1)}), bf16[16,4096]{1,0:T(8,128)(2,1)}) %reduce-scatter.3.cloned.1.call-update) | async-done | bytes 131088 | tf_op jit(solution)/shard_map/reduce_scatter | solution.py:96
  769.3 16.9 %all_to_all.10 = bf16[16,4,4096]{2,1,0:T(4,128)(2,1)S(1)} all-to-all(bf16[16,4,4096]{2,1,0:T(4,128)(2,1)S(1)} %reshape.78), channel_id=1, replica_groups=mesh['seq'=16,'expert'=8] {'seq'}, dimensions={0} | all-to-all | bytes 1048576 | tf_op jit(solution)/shard_map/all_to_all | solution.py:113
  787.2 29.3 %all-gather.11.cloned.1.call-done = bf16[8,64,4096]{2,1,0:T(8,128)(2,1)} async-done(((bf16[1,64,4096]{2,1,0:T(8,128)(2,1)}), bf16[8,64,4096]{2,1,0:T(8,128)(2,1)}) %all-gather.11.cloned.1.call-update) | async-done | bytes 4194320 | tf_op jit(solution)/shard_map/all_gather | solution.py:116
  816.5 10.1 %fusion.6 = f32[512,896]{1,0:T(8,128)} fusion(bf16[512,4096]{1,0:T(8,128)(2,1)} %bitcast.51, bf16[1,4096,896]{2,1,0:T(8,128)(2,1)} %param.33), kind=kOutput, calls=%fused_computation.9 | convolution fusion | flops 3758096384 | bytes 13369344 | tf_op jit(solution)/shard_map/dot_general | solution.py:119
  826.6 16.7 %fusion.8 = bf16[512,4096]{1,0:T(8,128)(2,1)} fusion(bf16[1,896,4096]{2,1,0:T(8,128)(2,1)} %param.35, f32[512,896]{1,0:T(8,128)} %fusion.6, bf16[512,4096]{1,0:T(8,128)(2,1)} %bitcast.52, bf16[1,4096,896]{2,1,0:T(8,128)(2,1)} %param.34), kind=kOutput, calls=%fused_computation.11 | convolution fusion | flops 7521042432 | bytes 24903680 | tf_op jit(solution)/shard_map/dot_general | solution.py:123
  843.3 38.0 %reduce-scatter.5.cloned.1.call-done = bf16[64,4096]{1,0:T(8,128)(2,1)} async-done(((bf16[512,4096]{1,0:T(8,128)(2,1)}), bf16[64,4096]{1,0:T(8,128)(2,1)}) %reduce-scatter.5.cloned.1.call-update) | async-done | bytes 524304 | tf_op jit(solution)/shard_map/reduce_scatter | solution.py:122
  883.3 7.1 all-to-all-start.1
  890.5 10.1 %all-to-all-done.1 = bf16[16,4,4096]{2,1,0:T(4,128)(2,1)S(1)} async-done(((bf16[16,4,4096]{2,1,0:T(4,128)(2,1)}), bf16[16,4,4096]{2,1,0:T(4,128)(2,1)S(1)}, u32[]{:S(2)}, u32[]{:S(2)}) %all-to-all-start.1) | async-done | bytes 524320 | tf_op jit(solution)/shard_map/all_to_all | solution.py:128
  (257 shorter events, 227.7 us)
Async XLA Ops:
  6.5 155.7 %copy-start = (bf16[1024,288]{0,1:T(8,128)(2,1)S(1)}, bf16[1024,288]{0,1:T(8,128)(2,1)}, u32[]{:S(2)}) copy-start(bf16[1024,288]{0,1:T(8,128)(2,1)} %param.24) | copy-start | bytes 1769476
  6.5 28.4 %all-gather.5.cloned.1.call-start = ((), (), s32[]{:S(2)}) async-start(), calls=%async_computation.4 | async-start | bytes 1179648 | tf_op jit(solution)/shard_map/all_gather | solution.py:49
  7.3 141.1 %all-gather.7.cloned.1.call-start = ((), (), s32[]{:S(2)}) async-start(), calls=%async_computation.5 | async-start | bytes 17825792 | tf_op jit(solution)/shard_map/all_gather | solution.py:55
  8.0 215.6 %all-reduce.30.cloned.1.call-start = ((), (), s32[]{:S(2)}) async-start(), calls=%async_computation.6 | async-start | bytes 131072 | tf_op jit(solution)/shard_map/psum | solution.py:68
  36.4 125.5 %copy-start.39 = (f32[1024]{0:T(1024)S(1)}, f32[1024]{0:T(1024)}, u32[]{:S(2)}) copy-start(f32[1024]{0:T(1024)} %param.23) | copy-start | bytes 12292
  36.4 187.1 %copy-start.42 = (bf16[256,1024]{1,0:T(8,128)(2,1)S(1)}, bf16[256,1024]{1,0:T(8,128)(2,1)}, u32[]{:S(2)}) copy-start(bf16[256,1024]{1,0:T(8,128)(2,1)} %param.25) | copy-start | bytes 1572868
  36.4 187.1 %copy-start.43 = (f32[1024]{0:T(1024)S(1)}, f32[1024]{0:T(1024)}, u32[]{:S(2)}) copy-start(f32[1024]{0:T(1024)} %param.26) | copy-start | bytes 12292
  156.9 68.0 %copy-start.37 = (f32[16,1024]{1,0:T(8,128)S(1)}, f32[16,1024]{1,0:T(8,128)}, u32[]{:S(2)}) copy-start(f32[16,1024]{1,0:T(8,128)} %param.27) | copy-start | bytes 196612
  156.9 5.0 collective-permute-start.1
  162.2 64.8 %copy-start.23 = (bf16[128,1024]{1,0:T(8,128)(2,1)}, bf16[128,1024]{1,0:T(8,128)(2,1)S(1)}, u32[]{:S(2)}) copy-start(bf16[128,1024]{1,0:T(8,128)(2,1)S(1)} %multiply_convert_fusion.1) | copy-start | bytes 786436
  163.2 557.3 %all-gather.9.cloned.1.call-start = ((), (), s32[]{:S(2)}) async-start(), calls=%async_computation.7 | async-start | bytes 8912896 | tf_op jit(solution)/shard_map/all_gather | solution.py:93
  163.8 602.9 %reduce-scatter.3.cloned.1.call-start = ((), (), s32[]{:S(2)}) async-start(), calls=%async_computation.8 | async-start | bytes 1179648 | tf_op jit(solution)/shard_map/reduce_scatter | solution.py:96
  561.5 144.9 %copy-start.28 = (f32[128,16]{1,0:T(8,128)S(1)}, f32[128,16]{1,0:T(8,128)}, u32[]{:S(2)}) copy-start(f32[128,16]{1,0:T(8,128)} %copy.42) | copy-start | bytes 24580
  598.8 5.0 collective-permute-start
  603.9 5.8 collective-permute-start
  609.7 5.9 collective-permute-start
  615.6 5.8 collective-permute-start
  621.5 5.8 collective-permute-start
  627.3 7.2 collective-permute-start
  634.5 8.1 collective-permute-start
  642.6 8.1 collective-permute-start
  650.7 7.9 collective-permute-start
  658.6 7.9 collective-permute-start
  666.6 8.0 collective-permute-start
  674.6 7.8 collective-permute-start
  682.5 7.9 collective-permute-start
  690.4 8.1 collective-permute-start
  698.5 7.9 collective-permute-start
  726.3 90.2 %all-gather.11.cloned.1.call-start = ((), (), s32[]{:S(2)}) async-start(), calls=%async_computation.9 | async-start | bytes 4718592 | tf_op jit(solution)/shard_map/all_gather | solution.py:116
  787.1 94.2 %reduce-scatter.5.cloned.1.call-start = ((), (), s32[]{:S(2)}) async-start(), calls=%async_computation.10 | async-start | bytes 4718592 | tf_op jit(solution)/shard_map/reduce_scatter | solution.py:122
  826.6 75.1 %copy-start.1 = (bf16[1024,288]{0,1:T(8,128)(2,1)S(1)}, bf16[1024,288]{0,1:T(8,128)(2,1)}, u32[]{:S(2)}) copy-start(bf16[1024,288]{0,1:T(8,128)(2,1)} %param.24) | copy-start | bytes 1769476
  883.3 17.2 %all-to-all-start.1 = ((bf16[16,4,4096]{2,1,0:T(4,128)(2,1)}), bf16[16,4,4096]{2,1,0:T(4,128)(2,1)S(1)}, u32[]{:S(2)}, u32[]{:S(2)}) async-start(bf16[16,4,4096]{2,1,0:T(4,128)(2,1)} %reshape.81), calls=%async_computation.3 | async-start | bytes 1048576 | tf_op jit(solution)/shard_map/all_to_all | solution.py:128
  (37 other events, 523.4 us)
Sparse Core Ops, SparseCore 0:
  9.1 25.7 all-gather.4
  37.0 111.3 all-gather.6
  163.4 60.1 all-reduce.29
  225.7 77.5 all-gather.8
  726.4 40.3 reduce-scatter.2
  787.2 29.2 all-gather.10
  843.4 37.8 reduce-scatter.4
where the time goes:
time: 924 us; the launch traced here: 909 us
  waiting for transfers between devices  327 us (35%)
  local copies, waits for them, and re-layouts  289 us (31%)
  other arithmetic  109 us (12%)
  starting transfers between devices  94.2 us (10%)
  matrix products  44.8 us (5%)
  blocking collectives  30.9 us (3%)
  between operations  14 us (2%)
    pad x24, local copies, waits for them, and re-layouts, per_device(): lax.associative_scan(combine_states, (decay, source), axis=0)  267 us
    all_gather x1, waiting for transfers between devices, per_device(): lax.all_gather(in_weight, 'seq', axis=1, tiled=True)  112 us
    ppermute x16, starting transfers between devices, from_behind(): return lax.ppermute(block, axis, route)  86.9 us
    psum x1, waiting for transfers between devices, per_device(): lax.psum(partial_value[:, :RANK].astype(jnp.bfloat16), 'expert')  44.8 us
    reduce_scatter x1, waiting for transfers between devices, per_device(): lax.psum_scatter(terms.astype(jnp.bfloat16), 'expert', scatter_dimension=...  39.7 us
    reduce_scatter x1, waiting for transfers between devices, per_device(): lax.psum_scatter(jnp.dot(act, w_down[0], preferred_element_type=jnp.float...  38 us
    add x12, other arithmetic, combine_states(): return (earlier[0] * later[0], later[0] * earlier[1] + later[1])  34.6 us
    add x12, other arithmetic, per_device(): lax.associative_scan(combine_states, (decay, source), axis=0)  33.2 us
  transfers between devices with their start and end apart: 24, of which 23 were waited for; matrix products, arithmetic and copies ran while one was open for 42% of the time, Pallas kernels for 0%

commit v1 on v0

--- a/solution.py
+++ b/solution.py
@@ -7,6 +7,13 @@
 CONV = 4
 RANK = 256
 TOP = 2
+
+
+def swapped_in(shard, axis, dim):
+    size = lax.axis_size(axis)
+    blocks = jnp.stack([shard for _ in range(size)])
+    blocks = lax.all_to_all(blocks, axis, split_axis=0, concat_axis=0)
+    return jnp.concatenate(blocks, axis=dim)
 
 
 def from_behind(block, axis, distance):
@@ -50,10 +57,7 @@
     local_tok = group.shape[0]
     normed = rms_norm(group, gain_mamba).astype(jnp.bfloat16)
     both = jnp.einsum(
-        "td,kdc->tkc",
-        normed,
-        lax.all_gather(in_weight, "seq", axis=1, tiled=True),
-        preferred_element_type=jnp.float32,
+        "td,kdc->tkc", normed, swapped_in(in_weight, "seq", 1), preferred_element_type=jnp.float32
     )
     xpart = both[:, 0]
     zpart = both[:, 1]

time: 924 us -> 1050 us (1.14)
  waiting for transfers between devices: 327 us -> 438 us
  local copies, waits for them, and re-layouts: 289 us -> 303 us
    all_to_all x0 -> x1, waiting for transfers between devices: none -> 221 us  [swapped_in(): blocks = lax.all_to_all(blocks, axis, split_axis=0, concat_axis=0)]
    all_gather x1 -> x0, waiting for transfers between devices: 112 us -> none  [per_device(): lax.all_gather(in_weight, 'seq', axis=1, tiled=True)]
  transfers between devices with their start and end apart: 24 -> 24, of which waited for: 23 -> 23; matrix products, arithmetic and copies ran while one was open for 42% -> 37% of each run, Pallas kernels for 0% -> 0%
where the time goes in v1:
time: 1050 us; the launch traced here: 1030 us
  waiting for transfers between devices  438 us (42%)
  local copies, waits for them, and re-layouts  303 us (29%)
  other arithmetic  108 us (10%)
  starting transfers between devices  99.7 us (9%)
  matrix products  38.8 us (4%)
  blocking collectives  30.1 us (3%)
  between operations  15.2 us (1%)
    pad x24, local copies, waits for them, and re-layouts, per_device(): lax.associative_scan(combine_states, (decay, source), axis=0)  267 us
    all_to_all x1, waiting for transfers between devices, swapped_in(): blocks = lax.all_to_all(blocks, axis, split_axis=0, concat_axis=0)  221 us
    ppermute x16, starting transfers between devices, from_behind(): return lax.ppermute(block, axis, route)  84.1 us
    psum x1, waiting for transfers between devices, per_device(): lax.psum(partial_value[:, :RANK].astype(jnp.bfloat16), 'expert')  47.5 us
    reduce_scatter x1, waiting for transfers between devices, per_device(): lax.psum_scatter(terms.astype(jnp.bfloat16), 'expert', scatter_dimension=...  39.7 us
    reduce_scatter x1, waiting for transfers between devices, per_device(): lax.psum_scatter(jnp.dot(act, w_down[0], preferred_element_type=jnp.float...  37.9 us
    add x12, other arithmetic, combine_states(): return (earlier[0] * later[0], later[0] * earlier[1] + later[1])  34.2 us
    add x12, other arithmetic, per_device(): lax.associative_scan(combine_states, (decay, source), axis=0)  33.1 us
  transfers between devices with their start and end apart: 24, of which 23 were waited for; matrix products, arithmetic and copies ran while one was open for 37% of the time, Pallas kernels for 0%

profile of v1, /device:TPU:0, one launch (start us, length us, event | category | flops | bytes accessed | tf_op | source)
XLA Modules:
  0.0 1034.3 jit_solution(18035692133829836670)
XLA Ops:
  7.4 6.9 stack.2
  14.3 8.3 all-to-all-start
  23.4 26.6 %all-gather.4.cloned.1.call-done = bf16[128,4096]{1,0:T(8,128)(2,1)} async-done(((bf16[16,4096]{1,0:T(8,128)(2,1)}), bf16[128,4096]{1,0:T(8,128)(2,1)}) %all-gather.4.cloned.1.call-update) | async-done | bytes 1048592 | tf_op jit(solution)/shard_map/all_gather | solution.py:56
  51.6 220.8 %all-to-all-done = bf16[16,2,256,1024]{3,2,1,0:T(8,128)(2,1)} async-done(((bf16[16,2,256,1024]{3,2,1,0:T(8,128)(2,1)}), bf16[16,2,256,1024]{3,2,1,0:T(8,128)(2,1)}, u32[]{:S(2)}, u32[]{:S(2)}) %all-to-all-start) | async-done | bytes 16777248 | tf_op jit(solution)/shard_map/all_to_all | solution.py:15
  272.4 8.3 copy.44
  288.0 13.2 %psum.14 = bf16[128,32]{0,1:T(8,128)(2,1)S(1)} all-reduce(bf16[128,32]{0,1:T(8,128)(2,1)S(1)} %slice.341), channel_id=1, replica_groups=mesh['seq'=16,'expert'=8] {'expert'}, use_global_device_ids=true, to_apply=%region_1.2 | all-reduce | flops 4096 | bytes 16384 | tf_op jit(solution)/shard_map/psum | solution.py:73
  302.0 47.5 %all-reduce.30.cloned.1.call-done = bf16[128,256]{0,1:T(8,128)(2,1)} async-done(((bf16[128,256]{0,1:T(8,128)(2,1)}), bf16[128,256]{0,1:T(8,128)(2,1)}) %all-reduce.30.cloned.1.call-update) | async-done | bytes 65552 | tf_op jit(solution)/shard_map/psum | solution.py:72
  359.6 10.8 %slice_add_fusion = (f32[64,16,1024]{2,1,0:T(8,128)S(1)}, f32[64,16,1024]{2,1,0:T(8,128)}) fusion(f32[128,16,1024]{2,1,0:T(8,128)} %copy-done.3, f32[128,16,1024]{2,1,0:T(8,128)} %copy-done.2), kind=kLoop, calls=%fused_computation.19 | loop fusion | flops 3145728 | bytes 25165824 | tf_op jit(solution)/shard_map/add | solution.py:31
  434.3 7.0 pad.108
  441.3 10.2 pad.109
  451.4 10.1 pad.95
  463.9 10.2 pad.94
  487.9 18.6 %pad.96 = f32[64,16,1024]{2,1,0:T(8,128)} pad(f32[32,16,1024]{2,1,0:T(8,128)} %pad_maximum_fusion.2, f32[]{:T(128)} %constant.13.clone.1), padding=0_1_1x0_0_0x0_0_0 | pad | bytes 6291460 | tf_op jit(solution)/shard_map/pad | solution.py:82
  506.6 12.0 %pad.97 = f32[64,16,1024]{2,1,0:T(8,128)} pad(f32[32,16,1024]{2,1,0:T(8,128)S(1)} %copy-done.16, f32[]{:T(128)} %constant.13.clone.1), padding=1_0_1x0_0_0x0_0_0 | pad | bytes 6291460 | tf_op jit(solution)/shard_map/pad | solution.py:82
  525.4 35.6 %pad.99 = f32[128,16,1024]{2,1,0:T(8,128)} pad(f32[64,16,1024]{2,1,0:T(8,128)} %add.257, f32[]{:T(128)} %constant.13.clone.1), padding=1_0_1x0_0_0x0_0_0 | pad | bytes 12582916 | tf_op jit(solution)/shard_map/pad | solution.py:82
  562.5 18.6 %pad.110 = f32[64,16,1024]{2,1,0:T(8,128)} pad(f32[32,16,1024]{2,1,0:T(8,128)} %pad_maximum_fusion.3, f32[]{:T(128)} %constant.13.clone.1), padding=0_1_1x0_0_0x0_0_0 | pad | bytes 6291460 | tf_op jit(solution)/shard_map/pad | solution.py:82
  581.1 12.0 %pad.111 = f32[64,16,1024]{2,1,0:T(8,128)} pad(f32[32,16,1024]{2,1,0:T(8,128)S(1)} %copy-done.15, f32[]{:T(128)} %constant.13.clone.1), padding=1_0_1x0_0_0x0_0_0 | pad | bytes 6291460 | tf_op jit(solution)/shard_map/pad | solution.py:82
  593.1 7.1 add.265
  601.7 7.4 fusion.12
  611.7 35.6 %pad.98 = f32[128,16,1024]{2,1,0:T(8,128)} pad(f32[64,16,1024]{2,1,0:T(8,128)} %pad_maximum_fusion, f32[]{:T(128)} %constant.13.clone.1), padding=0_1_1x0_0_0x0_0_0 | pad | bytes 12582916 | tf_op jit(solution)/shard_map/pad | solution.py:82
  647.3 35.6 %pad.113 = f32[128,16,1024]{2,1,0:T(8,128)} pad(f32[64,16,1024]{2,1,0:T(8,128)} %add.265, f32[]{:T(128)} %constant.13.clone.1), padding=1_0_1x0_0_0x0_0_0 | pad | bytes 12582916 | tf_op jit(solution)/shard_map/pad | solution.py:82
  687.6 35.6 %pad.112 = f32[128,16,1024]{2,1,0:T(8,128)} pad(f32[64,16,1024]{2,1,0:T(8,128)} %pad_maximum_fusion.1, f32[]{:T(128)} %constant.13.clone.1), padding=0_1_1x0_0_0x0_0_0 | pad | bytes 12582916 | tf_op jit(solution)/shard_map/pad | solution.py:82
  724.9 107.1 %while.11 = (s32[]{:T(128)}, f32[16,1024]{1,0:T(8,128)S(1)}, f32[16,1024]{1,0:T(8,128)S(1)}, f32[16,1024]{1,0:T(8,128)S(1)}, s32[]{:T(128)}, /*index=5*/s32[]{:T(128)}) while((s32[]{:T(128)}, f32[16,1024]{1,0:T(8,128)S(1)}, f32[16,1024]{1,0:T(8,128)S(1)}, f32[16,1024]{1,0:T(8,128)S(1)}, s32[]{:T(128)}, /*index=5*/s32[]{:T(128)}) %tuple.47), condition=%wide.region_4.5_spmd.clone, body=%wide.region_3.4_spmd.clone.sunk | while | flops 81923 | bytes 458871 | solution.py:91
  832.1 14.0 %multiply_reduce_fusion = f32[128,1024]{1,0:T(8,128)S(1)} fusion(f32[128,16,1024]{2,1,0:T(8,128)} %pad.112, f32[128,16,1024]{2,1,0:T(8,128)} %pad.113, f32[128,16,1024]{2,1,0:T(8,128)} %pad.98, f32[128,16,1024]{2,1,0:T(8,128)} %pad.99, f32[16,1024]{1,0:T(8,128)S(1)} %get-tuple-element.27, f32[128,16]{1,0:T(8,128)S(1)} %copy-done.29), kind=kLoop, calls=%fused_computation.3 | loop fusion | flops 12451840 | bytes 34152448 | tf_op jit(solution)/shard_map/reduce_sum | solution.py:93
  852.7 39.7 %reduce-scatter.3.cloned.1.call-done = bf16[16,4096]{1,0:T(8,128)(2,1)} async-done(((bf16[128,4096]{1,0:T(8,128)(2,1)}), bf16[16,4096]{1,0:T(8,128)(2,1)}) %reduce-scatter.3.cloned.1.call-update) | async-done | bytes 131088 | tf_op jit(solution)/shard_map/reduce_scatter | solution.py:100
  894.9 17.0 %all_to_all.15 = bf16[16,4,4096]{2,1,0:T(4,128)(2,1)S(1)} all-to-all(bf16[16,4,4096]{2,1,0:T(4,128)(2,1)S(1)} %reshape.88), channel_id=1, replica_groups=mesh['seq'=16,'expert'=8] {'seq'}, dimensions={0} | all-to-all | bytes 1048576 | tf_op jit(solution)/shard_map/all_to_all | solution.py:117
  912.9 29.3 %all-gather.8.cloned.1.call-done = bf16[8,64,4096]{2,1,0:T(8,128)(2,1)} async-done(((bf16[1,64,4096]{2,1,0:T(8,128)(2,1)}), bf16[8,64,4096]{2,1,0:T(8,128)(2,1)}) %all-gather.8.cloned.1.call-update) | async-done | bytes 4194320 | tf_op jit(solution)/shard_map/all_gather | solution.py:120
  942.2 10.1 fusion.6
  952.3 16.6 %fusion.8 = bf16[512,4096]{1,0:T(8,128)(2,1)} fusion(bf16[1,896,4096]{2,1,0:T(8,128)(2,1)} %param.35, f32[512,896]{1,0:T(8,128)} %fusion.6, bf16[512,4096]{1,0:T(8,128)(2,1)} %bitcast.55, bf16[1,4096,896]{2,1,0:T(8,128)(2,1)} %param.34), kind=kOutput, calls=%fused_computation.11 | convolution fusion | flops 7521042432 | bytes 24903680 | tf_op jit(solution)/shard_map/dot_general | solution.py:127
  969.0 37.9 %reduce-scatter.5.cloned.1.call-done = bf16[64,4096]{1,0:T(8,128)(2,1)} async-done(((bf16[512,4096]{1,0:T(8,128)(2,1)}), bf16[64,4096]{1,0:T(8,128)(2,1)}) %reduce-scatter.5.cloned.1.call-update) | async-done | bytes 524304 | tf_op jit(solution)/shard_map/reduce_scatter | solution.py:126
  1009.0 7.0 all-to-all-start.2
  1016.0 10.1 all-to-all-done.2
  (264 shorter events, 239.4 us)
Async XLA Ops:
  7.4 279.0 %copy-start = (bf16[1024,288]{0,1:T(8,128)(2,1)S(1)}, bf16[1024,288]{0,1:T(8,128)(2,1)}, u32[]{:S(2)}) copy-start(bf16[1024,288]{0,1:T(8,128)(2,1)} %param.24) | copy-start | bytes 1769476
  14.3 258.0 %all-to-all-start = ((bf16[16,2,256,1024]{3,2,1,0:T(8,128)(2,1)}), bf16[16,2,256,1024]{3,2,1,0:T(8,128)(2,1)}, u32[]{:S(2)}, u32[]{:S(2)}) async-start(bf16[16,2,256,1024]{3,2,1,0:T(8,128)(2,1)} %stack.2), calls=%async_computation | async-start | bytes 33554432 | tf_op jit(solution)/shard_map/all_to_all | solution.py:15
  22.6 27.4 %all-gather.4.cloned.1.call-start = ((), (), s32[]{:S(2)}) async-start(), calls=%async_computation.5 | async-start | bytes 1179648 | tf_op jit(solution)/shard_map/all_gather | solution.py:56
  23.4 326.2 %all-reduce.30.cloned.1.call-start = ((), (), s32[]{:S(2)}) async-start(), calls=%async_computation.6 | async-start | bytes 131072 | tf_op jit(solution)/shard_map/psum | solution.py:72
  280.6 68.9 %copy-start.45 = (bf16[256,1024]{1,0:T(8,128)(2,1)S(1)}, bf16[256,1024]{1,0:T(8,128)(2,1)}, u32[]{:S(2)}) copy-start(bf16[256,1024]{1,0:T(8,128)(2,1)} %param.25) | copy-start | bytes 1572868
  280.7 68.9 %copy-start.46 = (f32[1024]{0:T(1024)S(1)}, f32[1024]{0:T(1024)}, u32[]{:S(2)}) copy-start(f32[1024]{0:T(1024)} %param.26) | copy-start | bytes 12292
  283.1 67.8 %copy-start.38 = (f32[16,1024]{1,0:T(8,128)S(1)}, f32[16,1024]{1,0:T(8,128)}, u32[]{:S(2)}) copy-start(f32[16,1024]{1,0:T(8,128)} %param.27) | copy-start | bytes 196612
  283.2 2.9 collective-permute-start.1
  286.4 66.6 %copy-start.24 = (bf16[128,1024]{1,0:T(8,128)(2,1)}, bf16[128,1024]{1,0:T(8,128)(2,1)S(1)}, u32[]{:S(2)}) copy-start(bf16[128,1024]{1,0:T(8,128)(2,1)S(1)} %multiply_convert_fusion.1) | copy-start | bytes 786436
  287.4 558.7 %all-gather.6.cloned.1.call-start = ((), (), s32[]{:S(2)}) async-start(), calls=%async_computation.7 | async-start | bytes 8912896 | tf_op jit(solution)/shard_map/all_gather | solution.py:97
  288.0 604.4 %reduce-scatter.3.cloned.1.call-start = ((), (), s32[]{:S(2)}) async-start(), calls=%async_computation.8 | async-start | bytes 1179648 | tf_op jit(solution)/shard_map/reduce_scatter | solution.py:100
  687.6 144.4 %copy-start.29 = (f32[128,16]{1,0:T(8,128)S(1)}, f32[128,16]{1,0:T(8,128)}, u32[]{:S(2)}) copy-start(f32[128,16]{1,0:T(8,128)} %copy.45) | copy-start | bytes 24580
  725.0 4.9 collective-permute-start
  729.9 5.9 collective-permute-start
  735.9 6.0 collective-permute-start
  741.9 5.8 collective-permute-start
  747.7 5.8 collective-permute-start
  753.5 6.7 collective-permute-start
  760.3 7.9 collective-permute-start
  768.2 8.1 collective-permute-start
  776.3 7.9 collective-permute-start
  784.2 7.9 collective-permute-start
  792.2 8.0 collective-permute-start
  800.2 7.8 collective-permute-start
  808.1 7.9 collective-permute-start
  816.0 8.1 collective-permute-start
  824.1 7.9 collective-permute-start
  851.8 90.4 %all-gather.8.cloned.1.call-start = ((), (), s32[]{:S(2)}) async-start(), calls=%async_computation.9 | async-start | bytes 4718592 | tf_op jit(solution)/shard_map/all_gather | solution.py:120
  912.8 94.1 %reduce-scatter.5.cloned.1.call-start = ((), (), s32[]{:S(2)}) async-start(), calls=%async_computation.10 | async-start | bytes 4718592 | tf_op jit(solution)/shard_map/reduce_scatter | solution.py:126
  952.3 74.9 %copy-start.1 = (bf16[1024,288]{0,1:T(8,128)(2,1)S(1)}, bf16[1024,288]{0,1:T(8,128)(2,1)}, u32[]{:S(2)}) copy-start(bf16[1024,288]{0,1:T(8,128)(2,1)} %param.24) | copy-start | bytes 1769476
  969.0 57.2 %copy-start.23 = (bf16[16,4096]{1,0:T(8,128)(2,1)S(1)}, bf16[16,4096]{1,0:T(8,128)(2,1)}, u32[]{:S(2)}) copy-start(bf16[16,4096]{1,0:T(8,128)(2,1)} %reduce-scatter.3.cloned.1.call-done) | copy-start | bytes 393220
  1009.0 17.1 %all-to-all-start.2 = ((bf16[16,4,4096]{2,1,0:T(4,128)(2,1)}), bf16[16,4,4096]{2,1,0:T(4,128)(2,1)S(1)}, u32[]{:S(2)}, u32[]{:S(2)}) async-start(bf16[16,4,4096]{2,1,0:T(4,128)(2,1)} %reshape.91), calls=%async_computation.4 | async-start | bytes 1048576 | tf_op jit(solution)/shard_map/all_to_all | solution.py:132
  (40 other events, 494.9 us)
Sparse Core Ops, SparseCore 0:
  25.2 24.8 all-gather.3
  287.5 61.9 all-reduce.29
  852.0 40.3 reduce-scatter.2
  913.0 29.2 all-gather.7
  969.1 37.7 reduce-scatter.4
Sparse Core Ops, SparseCore 1:
  290.2 79.9 all-gather.5
